TPU v7x, 32 devices: a whole 2x2x4 slice. The times are simulated.
32 devices in a mesh: box: 16 (over z, y, x), samp: 2 (over core).
Axes of the slice: x: 2, y: 2, z: 4, core: 2. Of those that a mesh axis runs over, the one named last changes fastest.
Arguments:
- currents: bfloat16 [128, 8, 128], P(('box', 'samp')), may hold values from -6 to 6
- radiation: bfloat16 [128, 2, 2, 512, 128], P(('box', 'samp')), may hold values from -0.1875 to 0.1875
- near_blocks: bfloat16 [128, 8, 2, 128, 128], P(('box', 'samp')), may hold values from -0.125 to 0.125
- near_src: int32 [128, 8], P(('box', 'samp')), may hold values from 0 to 127, as said below
- leaf_parent: int32 [128], P('box'), may hold values from 0 to 255, as said below
- leaf_shift: int32 [128], P('box'), may hold values from 0 to 7
- shift_table: bfloat16 [8, 2, 8192], P(None, None, 'samp'), may hold values from -4 to 4
- interp_idx: int32 [64, 2], P('samp'), may hold values from 0 to 3, as said below
- interp_val: bfloat16 [64, 2, 128, 128], P('samp'), may hold values from -0.375 to 0.375
- top_src: int32 [256, 16], P('box'), may hold values from 0 to 255, as said below
- top_disp: int32 [256, 16], P('box'), may hold values from 0 to 31
- trans_table: bfloat16 [32, 2, 8192], P(None, None, 'samp'), may hold values from -1 to 1
Outputs:
- matvec: float32 [128, 8, 128], P(('box', 'samp'))
Inputs may be any that keep to these rules, and one draw needn't show every extreme that they name: `near_src`: entry 0 of a leaf's row is the leaf itself; every entry lies in the 4 leaves of the leaf's own device or of the devices just before and after it in box+samp order (leaves numbered box-major), and these ends are reached. `leaf_parent`: the parent of leaf l lies in its box group: its value divided by 16 equals l divided by 8. `interp_idx`: the 2 entries of a row differ. `top_src`: a source of top box t is another box of t's group (t // 16), or one of the last 8 boxes of the group before it, or one of the first 8 boxes of the group after it; both rims are reached.
All inputs are finite; a program needn't handle non-finite values.
Results may differ from a plain program's by a relative error of at most 0.013.
Values may be sent and summed in bfloat16 or wider, within the bound.
No kernel may reach another device: no remote copies, remote signals or barrier semaphores. Data moves between devices by JAX's collectives and lax.ppermute only.
A program may use at most 64 MiB of HBM per device.

v0:
```python
import functools

import jax
import jax.numpy as jnp
from jax import lax
from jax.experimental import pallas as pl
from jax.experimental.pallas import tpu as pltpu
from jax.sharding import PartitionSpec as P

F32 = jnp.float32
BF16 = jnp.bfloat16
HBM = pl.BlockSpec(memory_space=pltpu.HBM)
VMEM = pl.BlockSpec(memory_space=pltpu.VMEM)
SMEM = pl.BlockSpec(memory_space=pltpu.SMEM)
NT = (((1,), (1,)), ((), ()))
LIMIT = 24 * 1024 * 1024


def params():
    return pltpu.CompilerParams(vmem_limit_bytes=LIMIT)


def pinned(*arrays):
    return [pltpu.with_memory_space_constraint(array, pltpu.HBM) for array in arrays]


def radiate_kernel(
    parent_hbm, shift_hbm, cur_hbm, rad_hbm, msg_ref, parent_ref, shift_ref, cur_ref, rad_ref, sem, *, top_count
):
    leaf_count, in_blocks = cur_ref.shape[0], msg_ref.shape[0]
    block = msg_ref.shape[2]
    half = cur_ref.shape[1] // 2
    group = parent_ref.shape[0]
    firsts = [
        pltpu.make_async_copy(src, dst, sem.at[leaf_count + n])
        for n, (src, dst) in enumerate(
            ((parent_hbm, parent_ref), (shift_hbm, shift_ref), (cur_hbm, cur_ref))
        )
    ]
    for copy in firsts:
        copy.start()
    copies = [
        pltpu.make_async_copy(rad_hbm.at[leaf], rad_ref.at[leaf], sem.at[leaf])
        for leaf in range(leaf_count)
    ]
    for copy in copies:
        copy.start()
    base = leaf_count * 4 * half
    lane = lax.broadcasted_iota(jnp.int32, (8, block), 1)
    line = lax.broadcasted_iota(jnp.int32, (8, block), 0)
    meta = jnp.zeros((8, block), jnp.int32)
    for copy in firsts:
        copy.wait()
    for member in range(group):
        pair = jnp.where(
            line == 0, lax.rem(parent_ref[member], top_count), shift_ref[member]
        )
        meta = jnp.where(lane == member, pair, meta)
    meta = meta.astype(F32)
    zero = jnp.zeros((half, cur_ref.shape[2]), F32)
    left = []
    for leaf in range(leaf_count):
        cur = cur_ref[leaf].astype(F32)
        real, imag = cur[:half], cur[half:]
        pieces = [
            jnp.concatenate(rows, axis=0).astype(BF16)
            for rows in (
                (real, zero, imag, zero),
                (-imag, zero, real, zero),
                (zero, real, zero, imag),
                (zero, -imag, zero, real),
            )
        ]
        left.append(jnp.concatenate(pieces, axis=1))
        row = base + leaf // in_blocks * 4 * half
        msg_ref[leaf % in_blocks, row : row + 4 * half, :] = jnp.concatenate(
            [cur, meta], axis=0
        ).astype(BF16)
    for leaf in range(leaf_count):
        copies[leaf].wait()
        right = jnp.concatenate(
            [rad_ref[leaf, p, r] for p in range(2) for r in range(2)], axis=1
        )
        out = lax.dot_general(left[leaf], right, NT, preferred_element_type=F32).astype(BF16)
        for b in range(in_blocks):
            msg_ref[b, leaf * 4 * half : (leaf + 1) * 4 * half, :] = out[
                :, b * block : (b + 1) * block
            ]


def raise_group(msg_ref, sids, idx_ref, val_ref, shift_ref, up_ref, base, rows):
    block = val_ref.shape[2]
    local_blocks = val_ref.shape[0]
    count = len(sids)
    width = min(4, local_blocks)

    def some(step, carry):
        for inner in range(width):
            b = step * width + inner
            left = jnp.concatenate(
                [
                    msg_ref[:, idx_ref[b, r], :rows, :].reshape(count * 16, block)
                    for r in range(2)
                ],
                axis=1,
            )
            right = jnp.concatenate([val_ref[b, 0], val_ref[b, 1]], axis=1)
            moved = lax.dot_general(left, right, NT, preferred_element_type=F32)
            for s, sid in enumerate(sids):
                real, imag = moved[s * 16 : s * 16 + 8], moved[s * 16 + 8 : s * 16 + 16]
                shift_real, shift_imag = shift_ref[2 * sid, b], shift_ref[2 * sid + 1, b]
                up_ref[base + s, 0, b] = real * shift_real - imag * shift_imag
                up_ref[base + s, 1, b] = real * shift_imag + imag * shift_real
        return carry

    lax.fori_loop(0, local_blocks // width, some, 0)


def spread_rows(src_ref, out_ref):
    count, local_blocks, block = src_ref.shape

    def one(index, carry):
        for b in range(local_blocks):
            out_ref[index, b] = jnp.broadcast_to(src_ref[index, b : b + 1, :], (8, block))
        return carry

    lax.fori_loop(0, count, one, 0)


def tables_kernel(
    idx_ref,
    sid_ref,
    here_ref,
    val_hbm,
    shift_ref,
    trans_ref,
    val_ref,
    dense_ref,
    wide_shift_ref,
    wide_trans_ref,
    up_ref,
    sem,
    *,
    rows,
):
    load = pltpu.make_async_copy(val_hbm, val_ref, sem)
    load.start()
    spread_rows(shift_ref, wide_shift_ref)
    load.wait()
    local_blocks, _, block, _ = val_ref.shape
    sids = [sid_ref[s] for s in range(sid_ref.shape[0])]
    raise_group(here_ref, sids, idx_ref, val_ref, wide_shift_ref, up_ref, 0, rows)

    def one(b, carry):
        first, second = idx_ref[b, 0], idx_ref[b, 1]
        zero = jnp.zeros((block, block), BF16)
        for c in range(dense_ref.shape[1] // block):
            dense_ref[pl.ds(pl.multiple_of(b * block, block), block), c * block : (c + 1) * block] = (
                jnp.where(first == c, val_ref[b, 0], jnp.where(second == c, val_ref[b, 1], zero))
            )
        return carry

    lax.fori_loop(0, local_blocks, one, 0)
    spread_rows(trans_ref, wide_trans_ref)


def meta_of(msg_ref, rows):
    return msg_ref[0, 0, rows : rows + 16, :].astype(F32)[8:10]


def raise_kernel(idx_ref, msg_ref, val_ref, shift_ref, up_ref, meta_ref, num_ref, sem, *, rows):
    group = up_ref.shape[0]
    meta = meta_of(msg_ref, rows)
    meta_ref[...] = jnp.concatenate([meta] * 4, axis=0).astype(jnp.int32)
    fetch = pltpu.make_async_copy(meta_ref, num_ref, sem)
    fetch.start()
    fetch.wait()
    sids = [num_ref[1, s] for s in range(group)]
    raise_group(msg_ref, sids, idx_ref, val_ref, shift_ref, up_ref, 0, rows)


def field_kernel(
    idx_ref,
    parent_ref,
    sid_ref,
    src_ref,
    disp_ref,
    here_ref,
    near_ref,
    far_ref,
    near_up_hbm,
    here_up_hbm,
    val_ref,
    dense_ref,
    shift_ref,
    trans_ref,
    *rest,
    n_samp,
    leaf_count,
    tile,
):
    outs = rest[:n_samp]
    (
        top_ref,
        inc_ref,
        down_ref,
        acc_ref,
        meta_ref,
        num_ref,
        box_ref,
        rep_ref,
        count_ref,
        slot_ref,
        coef_ref,
        sem,
    ) = rest[n_samp:]
    block = val_ref.shape[2]
    local_blocks = val_ref.shape[0]
    leaves = top_ref.shape[0]
    group = leaves // 3
    rows = 16 * leaf_count
    top_count, entries = src_ref.shape
    where = lax.axis_index("box")
    me = lax.axis_index("samp")
    turned = jnp.where(me == 1, 1, 0) if n_samp == 2 else jnp.int32(0)
    bases = (1, 2 * turned, 2 - 2 * turned)

    moves = [
        pltpu.make_async_copy(src, top_ref.at[pl.ds(g * group, group)], sem.at[1 + g])
        for g, src in enumerate((here_up_hbm, near_up_hbm))
    ]
    lines = [meta_of(ref, rows) for ref in (here_ref, near_ref, far_ref)]
    meta_ref[...] = jnp.concatenate(lines + lines[:1], axis=0).astype(jnp.int32)
    fetch = pltpu.make_async_copy(meta_ref, num_ref, sem.at[0])
    fetch.start()
    for move in moves:
        move.start()
    for box in range(3 * top_count):
        box_ref[box] = -1
    fetch.wait()
    sids = [num_ref[5, s] for s in range(group)]
    raise_group(far_ref, sids, idx_ref, val_ref, shift_ref, top_ref, 2 * group, rows)
    boxes = [
        num_ref[2 * (s // group), s % group] + bases[s // group] * top_count for s in range(leaves)
    ]
    for s in reversed(range(leaves)):
        box_ref[boxes[s]] = s
    for s in range(leaves):
        rep_ref[s] = box_ref[boxes[s]]

    def listing(leaf, carry):
        parent = parent_ref[leaf] - where * top_count
        count = jnp.int32(0)
        slots = [box_ref[src_ref[parent, j] - (where - 1) * top_count] for j in range(entries)]
        coefs = [2 * disp_ref[parent, j] for j in range(entries)]
        for slot, coef in zip(slots, coefs):
            slot_ref[leaf, count] = slot
            coef_ref[leaf, count] = coef
            count += (slot >= 0).astype(jnp.int32)
        count_ref[leaf] = count
        return carry

    lax.fori_loop(0, group, listing, 0)
    for move in moves:
        move.wait()

    def merge(s, carry):
        rep = rep_ref[s]

        @pl.when(rep != s)
        def _():
            top_ref[rep] = top_ref[rep] + top_ref[s]

        return carry

    lax.fori_loop(0, leaves, merge, 0)

    def target(leaf, carry):
        @pl.when(rep_ref[leaf] == leaf)
        def _():
            for t in range(local_blocks // tile):

                def entry(n, total):
                    slot, coef = slot_ref[leaf, n], coef_ref[leaf, n]
                    real, imag = list(total[:tile]), list(total[tile:])
                    for b in range(tile):
                        place = t * tile + b
                        coef_real, coef_imag = trans_ref[coef, place], trans_ref[coef + 1, place]
                        src_real, src_imag = top_ref[slot, 0, place], top_ref[slot, 1, place]
                        real[b] += coef_real * src_real - coef_imag * src_imag
                        imag[b] += coef_real * src_imag + coef_imag * src_real
                    return tuple(real + imag)

                zero = jnp.zeros((8, block), F32)
                total = lax.fori_loop(0, count_ref[leaf], entry, (zero,) * (2 * tile))
                for b in range(tile):
                    inc_ref[leaf, 0, t * tile + b] = total[b]
                    inc_ref[leaf, 1, t * tile + b] = total[tile + b]

        return carry

    lax.fori_loop(0, group, target, 0)

    def lower(leaf, carry):
        sid = 2 * sid_ref[leaf]
        rep = rep_ref[leaf]
        start = pl.multiple_of(leaf * 16, 16)
        for b in range(local_blocks):
            shift_real, shift_imag = shift_ref[sid, b], shift_ref[sid + 1, b]
            real, imag = inc_ref[rep, 0, b], inc_ref[rep, 1, b]
            down = jnp.concatenate(
                [
                    shift_real * real + shift_imag * imag,
                    shift_real * imag - shift_imag * real,
                ],
                axis=0,
            )
            down_ref[pl.ds(start, 16), b * block : (b + 1) * block] = down.astype(BF16)
        return carry

    lax.fori_loop(0, group, lower, 0)
    acc_ref[...] = jnp.dot(down_ref[...], dense_ref[...], preferred_element_type=F32)
    for d, out in enumerate(outs):
        owner = lax.rem(me + d, n_samp)
        start = pl.multiple_of(owner * rows, rows)
        for c in range(out.shape[0]):
            out[c] = acc_ref[pl.ds(start, rows), c * block : (c + 1) * block].astype(BF16)


def near_kernel(src_ref, here_ref, first_ref, second_ref, near_hbm, out_ref, cur_ref, near_ref, sem, *, rows, n_samp):
    leaf_count, near = near_ref.shape[:2]
    in_blocks = here_ref.shape[1]
    group = n_samp * leaf_count
    copies = [
        pltpu.make_async_copy(near_hbm.at[leaf], near_ref.at[leaf], sem.at[leaf])
        for leaf in range(leaf_count)
    ]
    for copy in copies:
        copy.start()
    where = lax.axis_index("box")
    turned = jnp.where(lax.axis_index("samp") == 1, 1, 0) if n_samp == 2 else jnp.int32(0)
    for place, ref in ((1, here_ref), (2 * turned, first_ref), (2 - 2 * turned, second_ref)):
        for leaf in range(group):
            samp, inner = leaf // leaf_count, leaf % leaf_count
            line = rows + inner // in_blocks * 16
            cur = ref[samp, inner % in_blocks, line : line + 16, :].astype(F32)
            cur_ref[place * group + leaf] = jnp.concatenate(
                [cur[:8], -cur[4:8], cur[:4]], axis=0
            ).astype(BF16)
    for leaf in range(leaf_count):
        left = jnp.concatenate(
            [cur_ref[src_ref[leaf, n] - (where - 1) * group] for n in range(near)], axis=1
        )
        copies[leaf].wait()
        out = [
            lax.dot_general(
                left,
                jnp.concatenate([near_ref[leaf, n, r] for n in range(near)], axis=1),
                NT,
                preferred_element_type=F32,
            )
            for r in range(2)
        ]
        out_ref[leaf] = out[0][:8] + out[1][8:]


def receive_kernel(near_ref, rad_ref, *rest):
    far_refs, out_ref = rest[:-1], rest[-1]
    leaf_count = out_ref.shape[0]
    far = far_refs[0][...].astype(F32)
    for ref in far_refs[1:]:
        far = far + ref[...].astype(F32)
    in_blocks = far.shape[0]
    unknowns = rad_ref.shape[4]
    depth = rad_ref.shape[1] * rad_ref.shape[2] * rad_ref.shape[3]
    for leaf in range(leaf_count):
        left = []
        for p in range(2):
            real = [far[b, leaf * 16 + p * 4 : leaf * 16 + p * 4 + 4] for b in range(in_blocks)]
            imag = [
                far[b, leaf * 16 + 8 + p * 4 : leaf * 16 + 12 + p * 4] for b in range(in_blocks)
            ]
            left += [jnp.concatenate(pair, axis=0) for pair in zip(real, imag)]
            left += [jnp.concatenate([i, -r], axis=0) for r, i in zip(real, imag)]
        wide = jnp.concatenate(left, axis=1).astype(BF16)
        right = rad_ref[leaf].reshape(depth, unknowns)
        out_ref[leaf] = near_ref[leaf] + jnp.dot(wide, right, preferred_element_type=F32)


def per_device(
    currents,
    radiation,
    near_blocks,
    near_src,
    leaf_parent,
    leaf_shift,
    shift_table,
    interp_idx,
    interp_val,
    top_src,
    top_disp,
    trans_table,
):
    n_samp = lax.axis_size("samp")
    n_box = lax.axis_size("box")
    leaf_count, comps, unknowns = currents.shape
    group = leaf_parent.shape[0]
    top_count, entries = top_src.shape
    local_blocks, _, block, _ = interp_val.shape
    in_blocks = radiation.shape[3] // block
    leaves = 3 * group
    rows = 16 * leaf_count
    extra = 16 * -(-leaf_count // in_blocks)
    tile = min(16, local_blocks)

    message = pl.pallas_call(
        functools.partial(radiate_kernel, top_count=top_count),
        out_shape=jax.ShapeDtypeStruct((in_blocks, rows + extra, block), BF16),
        in_specs=[HBM] * 4,
        out_specs=VMEM,
        scratch_shapes=[
            pltpu.SMEM(leaf_parent.shape, jnp.int32),
            pltpu.SMEM(leaf_shift.shape, jnp.int32),
            pltpu.VMEM(currents.shape, BF16),
            pltpu.VMEM(radiation.shape, BF16),
            pltpu.SemaphoreType.DMA((leaf_count + 3,)),
        ],
        compiler_params=params(),
        name="radiate",
    )(*pinned(leaf_parent, leaf_shift, currents, radiation))

    here = lax.all_gather(message, "samp", axis=0)
    last = n_samp - 1
    swap = []
    for box in range(n_box - 1):
        low, high = box * n_samp + last, (box + 1) * n_samp
        swap += [(low, high), (high, low)]
    beyond = lax.ppermute(here, ("box", "samp"), swap)
    shift_rows = shift_table.astype(F32).reshape(-1, local_blocks, block)
    trans_rows = trans_table.astype(F32).reshape(-1, local_blocks, block)
    up_shape = pltpu.VMEM((group, 2, local_blocks, 8, block), F32)
    work = 2 * group * 16 * 2 * block * local_blocks * block
    values, dense, wide_shift, wide_trans, here_up = pl.pallas_call(
        functools.partial(tables_kernel, rows=rows),
        out_shape=[
            pltpu.VMEM(interp_val.shape, BF16),
            pltpu.VMEM((local_blocks * block, in_blocks * block), BF16),
            pltpu.VMEM((shift_rows.shape[0], local_blocks, 8, block), F32),
            pltpu.VMEM((trans_rows.shape[0], local_blocks, 8, block), F32),
            up_shape,
        ],
        in_specs=[SMEM, SMEM, VMEM, HBM, VMEM, VMEM],
        out_specs=[VMEM] * 5,
        scratch_shapes=[pltpu.SemaphoreType.DMA],
        compiler_params=params(),
        cost_estimate=pl.CostEstimate(flops=work, bytes_accessed=1 << 24, transcendentals=0),
        name="tables",
    )(interp_idx, leaf_shift, here, *pinned(interp_val), shift_rows, trans_rows)
    beyond, values = lax.optimization_barrier((beyond, values))
    if n_samp == 2:
        first = beyond
        second = lax.ppermute(beyond, "samp", [(0, 1), (1, 0)])
    else:
        ends = lax.all_gather(beyond, "samp", axis=0)
        first, second = ends[0], ends[n_samp - 1]
    numbers = [pltpu.VMEM((8, block), jnp.int32), pltpu.SMEM((8, block), jnp.int32)]
    first_up = pl.pallas_call(
        functools.partial(raise_kernel, rows=rows),
        out_shape=up_shape,
        in_specs=[SMEM] + [VMEM] * 3,
        out_specs=VMEM,
        scratch_shapes=numbers + [pltpu.SemaphoreType.DMA],
        compiler_params=params(),
        cost_estimate=pl.CostEstimate(flops=work, bytes_accessed=1 << 23, transcendentals=0),
        name="raise",
    )(interp_idx, first, values, wide_shift)

    fars = pl.pallas_call(
        functools.partial(field_kernel, n_samp=n_samp, leaf_count=leaf_count, tile=tile),
        out_shape=[jax.ShapeDtypeStruct((in_blocks, rows, block), BF16)] * n_samp,
        in_specs=[SMEM] * 5 + [VMEM] * 9,
        out_specs=[VMEM] * n_samp,
        scratch_shapes=[
            pltpu.VMEM((leaves, 2, local_blocks, 8, block), F32),
            pltpu.VMEM((group, 2, local_blocks, 8, block), F32),
            pltpu.VMEM((group * 16, local_blocks * block), BF16),
            pltpu.VMEM((group * 16, in_blocks * block), F32),
            *numbers,
            pltpu.SMEM((3 * top_count,), jnp.int32),
            pltpu.SMEM((leaves,), jnp.int32),
            pltpu.SMEM((group,), jnp.int32),
            pltpu.SMEM((group, entries), jnp.int32),
            pltpu.SMEM((group, entries), jnp.int32),
            pltpu.SemaphoreType.DMA((3,)),
        ],
        compiler_params=params(),
        name="field",
    )(
        interp_idx,
        leaf_parent,
        leaf_shift,
        top_src,
        top_disp,
        here,
        first,
        second,
        first_up,
        here_up,
        values,
        dense,
        wide_shift,
        wide_trans,
    )
    received = [fars[0]] + [
        lax.ppermute(fars[d], "samp", [(i, (i + d) % n_samp) for i in range(n_samp)])
        for d in range(1, n_samp)
    ]
    near_out = pl.pallas_call(
        functools.partial(near_kernel, rows=rows, n_samp=n_samp),
        out_shape=jax.ShapeDtypeStruct((leaf_count, comps, unknowns), F32),
        in_specs=[SMEM, VMEM, VMEM, VMEM, HBM],
        out_specs=VMEM,
        scratch_shapes=[
            pltpu.VMEM((leaves, 16, block), BF16),
            pltpu.VMEM(near_blocks.shape, BF16),
            pltpu.SemaphoreType.DMA((leaf_count,)),
        ],
        compiler_params=params(),
        name="near",
    )(near_src, here, first, second, near_blocks)
    return pl.pallas_call(
        receive_kernel,
        out_shape=jax.ShapeDtypeStruct((leaf_count, comps, unknowns), F32),
        in_specs=[VMEM] * (2 + n_samp),
        out_specs=VMEM,
        compiler_params=params(),
        name="receive",
    )(near_out, radiation, *received)


def solution(mesh):
    placed = (
        P(("box", "samp"), None, None),
        P(("box", "samp"), None, None, None, None),
        P(("box", "samp"), None, None, None, None),
        P(("box", "samp"), None),
        P("box"),
        P("box"),
        P(None, None, "samp"),
        P("samp", None),
        P("samp", None, None, None),
        P("box", None),
        P("box", None),
        P(None, None, "samp"),
    )
    return jax.shard_map(
        per_device,
        mesh=mesh,
        in_specs=placed,
        out_specs=P(("box", "samp"), None, None),
        check_vma=False,
    )
```

profile of v0, /device:TPU:15, one launch (start us, length us, event | category | flops | bytes accessed | tf_op | source)
XLA Modules:
  0.0 32.8 jit_solution(6149943702695271866)
XLA Ops:
  0.0 0.0 copy-start.8
  0.0 2.2 %radiate.1 = bf16[4,80,128]{2,1,0:T(8,128)(2,1)S(1)} custom-call(s32[8]{0:T(128)} %parent_ref.1, s32[8]{0:T(128)} %sid_ref.3, bf16[4,8,128]{2,1,0:T(8,128)(2,1)} %cur_hbm.1, bf16[4,2,2,512,128]{4,3,2,1,0:T(8,128)(2,1)} %rad_ref.1), custom_call_target="tpu_custom_call" | custom-call | tf_op jit(solution)/shard_map/radiate/pallas_call | solution.py:416
  2.2 2.2 %all-gather = bf16[8,80,128]{2,1,0:T(8,128)(2,1)S(1)} all-gather(bf16[4,80,128]{2,1,0:T(8,128)(2,1)S(1)} %radiate.1), channel_id=2, replica_groups=mesh['box'=16,'samp'=2] {'samp'}, dimensions={0}, use_global_device_ids=true | all-gather | bytes 245760 | tf_op jit(solution)/shard_map/all_gather | solution.py:432
  4.5 3.3 %collective-permute-start = (bf16[2,4,80,128]{3,2,1,0:T(8,128)(2,1)S(1)}, bf16[2,4,80,128]{3,2,1,0:T(8,128)(2,1)S(1)}, u32[]{:S(2)}, u32[]{:S(2)}) collective-permute-start(bf16[2,4,80,128]{3,2,1,0:T(8,128)(2,1)S(1)} %bitcast.1), channel_id=1, source_target_pairs={{1,2},{2,1},{3,4},{4,3},{5,6},{6,5},{7,8},{8,7},{9,10},{10,9},{11,... | collective-permute-start | bytes 491528 | tf_op jit(solution)/shard_map/ppermute | solution.py:438
  7.8 0.0 copy-done.9
  7.8 0.1 copy.16.idx_ref
  7.9 0.0 copy-done.7
  7.9 0.3 %reshape.17.trans_ref = f32[64,32,128]{2,1,0:T(8,128)S(1)} reshape(bf16[32,2,4096]{2,1,0:T(2,128)(2,1)S(1)} %copy-done.7) | data formatting | bytes 1572864 | tf_op jit(solution)/shard_map/reshape | solution.py:440
  8.3 0.0 copy-done.8
  8.3 0.1 reshape.15.shift_ref
  8.4 0.0 copy-done.4
  8.4 6.3 %tables.1 = (bf16[32,2,128,128]{3,2,1,0:T(8,128)(2,1)S(1)}, bf16[4096,512]{1,0:T(8,128)(2,1)S(1)}, f32[16,32,8,128]{3,2,1,0:T(8,128)S(1)}, f32[64,32,8,128]{3,2,1,0:T(8,128)S(1)}, f32[8,2,32,8,128]{4,3,2,1,0:T(8,128)S(1)}) custom-call(s32[32,2]{1,0:T(8,128)S(1)} %copy.16.idx_ref, s32[8]{0:T(128)S(1)} %copy-done.4, bf16[2,4,80,128]{3,2,1,0:T(8,128)(2,1)S(1)} %bitcast.2, ...), custom_call_target="tpu_custom_call" | custom-call | flops 268435456 | bytes 16777216 | tf_op jit(solution)/shard_map/tables/pallas_call | solution.py:443
  14.7 0.0 collective-permute-done.first_ref.msg_ref.near_ref
  14.7 0.1 collective-permute-start.1
  14.8 0.0 copy-start.2
  14.8 0.0 copy-start.3
  14.8 0.0 copy-start.6
  14.8 3.3 %raise.1.near_up_hbm = f32[8,2,32,8,128]{4,3,2,1,0:T(8,128)S(1)} custom-call(s32[32,2]{1,0:T(8,128)S(1)} %copy.16.idx_ref, bf16[2,4,80,128]{3,2,1,0:T(8,128)(2,1)S(1)} %collective-permute-done.first_ref.msg_ref.near_ref, bf16[32,2,128,128]{3,2,1,0:T(8,128)(2,1)S(1)} %get-tuple-element.16.val_ref, f32[16,32,8,128]{3,2,1,0:T(8,128)S(1)} %get-tuple-element.17.shift_ref), custom_call_target="tpu_custom_call" | custom-call | flops 268435456 | bytes 8388608 | tf_op jit(solution)/shard_map/raise/pallas_call | solution.py:467
  18.2 0.0 collective-permute-done.1.second_ref.far_ref
  18.2 0.0 copy-done.2
  18.2 0.0 copy-done.3
  18.2 0.0 copy-done.6
  18.2 0.0 copy-start.1
  18.2 0.0 copy-start.5
  18.2 11.2 %field.1 = (bf16[4,64,128]{2,1,0:T(8,128)(2,1)S(1)}, bf16[4,64,128]{2,1,0:T(8,128)(2,1)S(1)}) custom-call(s32[32,2]{1,0:T(8,128)S(1)} %copy.16.idx_ref, s32[8]{0:T(128)S(1)} %copy-done.6, s32[8]{0:T(128)S(1)} %copy-done.4, s32[16,16]{1,0:T(8,128)S(1)} %copy-done.2, s32[16,16]{1,0:T(8,128)S(1)} %copy-done.3, bf16[2,4,80,128]{3,2,1,0:T(8,128)(2,1)S(1)} %bitcast.3, ...), custom_call_target="tpu_custom_call" | custom-call | tf_op jit(solution)/shard_map/field/pallas_call | solution.py:478
  29.4 0.0 copy-start
  29.4 0.5 %collective-permute-start.2 = (bf16[4,64,128]{2,1,0:T(8,128)(2,1)S(1)}, bf16[4,64,128]{2,1,0:T(8,128)(2,1)S(1)}, u32[]{:S(2)}, u32[]{:S(2)}) collective-permute-start(bf16[4,64,128]{2,1,0:T(8,128)(2,1)S(1)} %get-tuple-element.22), channel_id=1, source_target_pairs={{0,1},{1,0},{2,3},{3,2},{4,5},{5,4},{6,7},{7,6},{8,9},{9,8},{10,11... | collective-permute-start | bytes 196616 | tf_op jit(solution)/shard_map/ppermute | solution.py:515
  29.9 0.0 copy-done.1
  29.9 0.0 copy-done.5
  29.9 1.8 %near.1.near_ref = f32[4,8,128]{2,1,0:T(8,128)S(1)} custom-call(s32[4,8]{1,0:T(4,128)S(1)} %copy-done.5, bf16[2,4,80,128]{3,2,1,0:T(8,128)(2,1)S(1)} %bitcast.4, bf16[2,4,80,128]{3,2,1,0:T(8,128)(2,1)S(1)} %collective-permute-done.first_ref.msg_ref.near_ref, bf16[2,4,80,128]{3,2,1,0:T(8,128)(2,1)S(1)} %collective-permute-done.1.second_ref.far_ref, ...), custom_call_target="tpu_custom_call" | custom-call | tf_op jit(solution)/shard_map/near/pallas_call | solution.py:518
  31.7 0.0 collective-permute-done.2.rest_1_
  31.8 1.0 %receive.1 = f32[4,8,128]{2,1,0:T(8,128)} custom-call(f32[4,8,128]{2,1,0:T(8,128)S(1)} %near.1.near_ref, bf16[4,2,2,512,128]{4,3,2,1,0:T(8,128)(2,1)S(1)} %copy-done, bf16[4,64,128]{2,1,0:T(8,128)(2,1)S(1)} %get-tuple-element.21.rest_0_, bf16[4,64,128]{2,1,0:T(8,128)(2,1)S(1)} %collective-permute-done.2.rest_1_), custom_call_target="tpu_custom_call" | custom-call | tf_op jit(solution)/shard_map/receive/pallas_call | solution.py:531
  (4 shorter events, 0.0 us)
Async XLA Ops:
  0.0 8.4 %copy-start.4 = (s32[8]{0:T(128)S(1)}, s32[8]{0:T(128)}, u32[]{:S(2)}) copy-start(s32[8]{0:T(128)} %sid_ref.3) | copy-start | bytes 100
  0.0 7.8 %copy-start.9 = (s32[32,2]{0,1:T(2,128)S(1)}, s32[32,2]{0,1:T(2,128)}, u32[]{:S(2)}) copy-start(s32[32,2]{0,1:T(2,128)} %param.19) | copy-start | bytes 772
  0.0 7.9 %copy-start.7 = (bf16[32,2,4096]{2,1,0:T(2,128)(2,1)S(1)}, bf16[32,2,4096]{2,1,0:T(2,128)(2,1)}, u32[]{:S(2)}) copy-start(bf16[32,2,4096]{2,1,0:T(2,128)(2,1)} %param.23) | copy-start | bytes 1572868
  0.0 8.3 %copy-start.8 = (bf16[8,2,4096]{2,1,0:T(2,128)(2,1)S(1)}, bf16[8,2,4096]{2,1,0:T(2,128)(2,1)}, u32[]{:S(2)}) copy-start(bf16[8,2,4096]{2,1,0:T(2,128)(2,1)} %param.18) | copy-start | bytes 393220
  4.5 10.2 %collective-permute-start = (bf16[2,4,80,128]{3,2,1,0:T(8,128)(2,1)S(1)}, bf16[2,4,80,128]{3,2,1,0:T(8,128)(2,1)S(1)}, u32[]{:S(2)}, u32[]{:S(2)}) collective-permute-start(bf16[2,4,80,128]{3,2,1,0:T(8,128)(2,1)S(1)} %bitcast.1), channel_id=1, source_target_pairs={{1,2},{2,1},{3,4},{4,3},{5,6},{6,5},{7,8},{8,7},{9,10},{10,9},{11,... | collective-permute-start | bytes 491528 | tf_op jit(solution)/shard_map/ppermute | solution.py:438
  14.7 3.4 %collective-permute-start.1 = (bf16[2,4,80,128]{3,2,1,0:T(8,128)(2,1)S(1)}, bf16[2,4,80,128]{3,2,1,0:T(8,128)(2,1)S(1)}, u32[]{:S(2)}, u32[]{:S(2)}) collective-permute-start(bf16[2,4,80,128]{3,2,1,0:T(8,128)(2,1)S(1)} %collective-permute-done.first_ref.msg_ref.near_ref), channel_id=1, source_target_pairs={{0,1},{1,0},{2,3},{3,2},{4,5},{5,4},{6,7},{7,6},{8,9},{9,8},{10,11... | collective-permute-start | bytes 491528 | tf_op jit(solution)/shard_map/ppermute | solution.py:462
  14.8 3.4 %copy-start.2 = (s32[16,16]{1,0:T(8,128)S(1)}, s32[16,16]{1,0:T(8,128)}, u32[]{:S(2)}) copy-start(s32[16,16]{1,0:T(8,128)} %src_ref.3) | copy-start | bytes 3076
  14.8 3.4 %copy-start.3 = (s32[16,16]{1,0:T(8,128)S(1)}, s32[16,16]{1,0:T(8,128)}, u32[]{:S(2)}) copy-start(s32[16,16]{1,0:T(8,128)} %disp_ref.1) | copy-start | bytes 3076
  14.8 3.4 %copy-start.6 = (s32[8]{0:T(128)S(1)}, s32[8]{0:T(128)}, u32[]{:S(2)}) copy-start(s32[8]{0:T(128)} %parent_ref.1) | copy-start | bytes 100
  18.2 11.7 %copy-start.1 = (bf16[4,8,2,128,128]{4,3,2,1,0:T(8,128)(2,1)S(1)}, bf16[4,8,2,128,128]{4,3,2,1,0:T(8,128)(2,1)}, u32[]{:S(2)}) copy-start(bf16[4,8,2,128,128]{4,3,2,1,0:T(8,128)(2,1)} %near_hbm.1) | copy-start | bytes 6291460
  18.2 11.7 %copy-start.5 = (s32[4,8]{1,0:T(4,128)S(1)}, s32[4,8]{1,0:T(4,128)}, u32[]{:S(2)}) copy-start(s32[4,8]{1,0:T(4,128)} %src_ref.2) | copy-start | bytes 388
  29.4 2.4 %copy-start = (bf16[4,2,2,512,128]{4,3,2,1,0:T(8,128)(2,1)S(1)}, bf16[4,2,2,512,128]{4,3,2,1,0:T(8,128)(2,1)}, u32[]{:S(2)}) copy-start(bf16[4,2,2,512,128]{4,3,2,1,0:T(8,128)(2,1)} %rad_ref.1) | copy-start | bytes 6291460
  29.4 2.3 %collective-permute-start.2 = (bf16[4,64,128]{2,1,0:T(8,128)(2,1)S(1)}, bf16[4,64,128]{2,1,0:T(8,128)(2,1)S(1)}, u32[]{:S(2)}, u32[]{:S(2)}) collective-permute-start(bf16[4,64,128]{2,1,0:T(8,128)(2,1)S(1)} %get-tuple-element.22), channel_id=1, source_target_pairs={{0,1},{1,0},{2,3},{3,2},{4,5},{5,4},{6,7},{7,6},{8,9},{9,8},{10,11... | collective-permute-start | bytes 196616 | tf_op jit(solution)/shard_map/ppermute | solution.py:515
where the time goes:
time: 32.6 us; the launch traced here: 32.8 us
  Pallas kernels  25.8 us (79%)
  starting transfers between devices  3.94 us (12%)
  blocking collectives  2.24 us (7%)
  local copies, waits for them, and re-layouts  0.57 us (2%)
    pallas_call x1, Pallas kernels, per_device(): pl.pallas_call(functools.partial(field_kernel, n_samp=n_samp, leaf_count=...  11.2 us
    pallas_call x1, Pallas kernels, per_device(): pl.pallas_call(functools.partial(tables_kernel, rows=rows), out_shape=[pl...  6.31 us
    ppermute x1, starting transfers between devices, per_device(): beyond = lax.ppermute(here, ('box', 'samp'), swap)  3.35 us
    pallas_call x1, Pallas kernels, per_device(): pl.pallas_call(functools.partial(raise_kernel, rows=rows), out_shape=up_s...  3.31 us
    all_gather x1, blocking collectives, per_device(): here = lax.all_gather(message, 'samp', axis=0)  2.24 us
    pallas_call x1, Pallas kernels, per_device(): pl.pallas_call(functools.partial(radiate_kernel, top_count=top_count), ou...  2.21 us
    pallas_call x1, Pallas kernels, per_device(): pl.pallas_call(functools.partial(near_kernel, rows=rows, n_samp=n_samp),...  1.79 us
    pallas_call x1, Pallas kernels, per_device(): pl.pallas_call(receive_kernel, out_shape=jax.ShapeDtypeStruct((leaf_count...  1 us
  transfers between devices with their start and end apart: 3, of which 0 were waited for; matrix products, arithmetic and copies ran while one was open for 2% of the time, Pallas kernels for 35%

commit v1 on v0

--- a/solution.py
+++ b/solution.py
@@ -88,32 +88,21 @@
             ]
 
 
-def raise_group(msg_ref, sids, idx_ref, val_ref, shift_ref, up_ref, base, rows):
-    block = val_ref.shape[2]
-    local_blocks = val_ref.shape[0]
-    count = len(sids)
-    width = min(4, local_blocks)
-
-    def some(step, carry):
-        for inner in range(width):
-            b = step * width + inner
-            left = jnp.concatenate(
-                [
-                    msg_ref[:, idx_ref[b, r], :rows, :].reshape(count * 16, block)
-                    for r in range(2)
-                ],
-                axis=1,
-            )
-            right = jnp.concatenate([val_ref[b, 0], val_ref[b, 1]], axis=1)
-            moved = lax.dot_general(left, right, NT, preferred_element_type=F32)
-            for s, sid in enumerate(sids):
-                real, imag = moved[s * 16 : s * 16 + 8], moved[s * 16 + 8 : s * 16 + 16]
-                shift_real, shift_imag = shift_ref[2 * sid, b], shift_ref[2 * sid + 1, b]
-                up_ref[base + s, 0, b] = real * shift_real - imag * shift_imag
-                up_ref[base + s, 1, b] = real * shift_imag + imag * shift_real
-        return carry
-
-    lax.fori_loop(0, local_blocks // width, some, 0)
+def lift_groups(refs, dense_ref, out_ref, rows):
+    left = jnp.concatenate(
+        [
+            jnp.concatenate([ref[samp, c, :rows, :] for c in range(ref.shape[1])], axis=1)
+            for ref in refs
+            for samp in range(ref.shape[0])
+        ],
+        axis=0,
+    )
+    samples = dense_ref.shape[0]
+    width = min(1024, samples)
+    for start in range(0, samples, width):
+        out_ref[:, start : start + width] = lax.dot_general(
+            left, dense_ref[start : start + width, :], NT, preferred_element_type=F32
+        )
 
 
 def spread_rows(src_ref, out_ref):
@@ -128,28 +117,13 @@
 
 
 def tables_kernel(
-    idx_ref,
-    sid_ref,
-    here_ref,
-    val_hbm,
-    shift_ref,
-    trans_ref,
-    val_ref,
-    dense_ref,
-    wide_shift_ref,
-    wide_trans_ref,
-    up_ref,
-    sem,
-    *,
-    rows,
+    idx_ref, val_hbm, shift_ref, trans_ref, dense_ref, wide_shift_ref, wide_trans_ref, val_ref, sem
 ):
     load = pltpu.make_async_copy(val_hbm, val_ref, sem)
     load.start()
     spread_rows(shift_ref, wide_shift_ref)
     load.wait()
     local_blocks, _, block, _ = val_ref.shape
-    sids = [sid_ref[s] for s in range(sid_ref.shape[0])]
-    raise_group(here_ref, sids, idx_ref, val_ref, wide_shift_ref, up_ref, 0, rows)
 
     def one(b, carry):
         first, second = idx_ref[b, 0], idx_ref[b, 1]
@@ -164,23 +138,15 @@
     spread_rows(trans_ref, wide_trans_ref)
 
 
+def lift_kernel(here_ref, near_ref, dense_ref, out_ref, *, rows):
+    lift_groups((here_ref, near_ref), dense_ref, out_ref, rows)
+
+
 def meta_of(msg_ref, rows):
     return msg_ref[0, 0, rows : rows + 16, :].astype(F32)[8:10]
 
 
-def raise_kernel(idx_ref, msg_ref, val_ref, shift_ref, up_ref, meta_ref, num_ref, sem, *, rows):
-    group = up_ref.shape[0]
-    meta = meta_of(msg_ref, rows)
-    meta_ref[...] = jnp.concatenate([meta] * 4, axis=0).astype(jnp.int32)
-    fetch = pltpu.make_async_copy(meta_ref, num_ref, sem)
-    fetch.start()
-    fetch.wait()
-    sids = [num_ref[1, s] for s in range(group)]
-    raise_group(msg_ref, sids, idx_ref, val_ref, shift_ref, up_ref, 0, rows)
-
-
 def field_kernel(
-    idx_ref,
     parent_ref,
     sid_ref,
     src_ref,
@@ -188,9 +154,7 @@
     here_ref,
     near_ref,
     far_ref,
-    near_up_hbm,
-    here_up_hbm,
-    val_ref,
+    lifted_ref,
     dense_ref,
     shift_ref,
     trans_ref,
@@ -202,6 +166,7 @@
     outs = rest[:n_samp]
     (
         top_ref,
+        last_ref,
         inc_ref,
         down_ref,
         acc_ref,
@@ -214,8 +179,8 @@
         coef_ref,
         sem,
     ) = rest[n_samp:]
-    block = val_ref.shape[2]
-    local_blocks = val_ref.shape[0]
+    block = here_ref.shape[3]
+    local_blocks = top_ref.shape[2]
     leaves = top_ref.shape[0]
     group = leaves // 3
     rows = 16 * leaf_count
@@ -225,21 +190,14 @@
     turned = jnp.where(me == 1, 1, 0) if n_samp == 2 else jnp.int32(0)
     bases = (1, 2 * turned, 2 - 2 * turned)
 
-    moves = [
-        pltpu.make_async_copy(src, top_ref.at[pl.ds(g * group, group)], sem.at[1 + g])
-        for g, src in enumerate((here_up_hbm, near_up_hbm))
-    ]
     lines = [meta_of(ref, rows) for ref in (here_ref, near_ref, far_ref)]
     meta_ref[...] = jnp.concatenate(lines + lines[:1], axis=0).astype(jnp.int32)
-    fetch = pltpu.make_async_copy(meta_ref, num_ref, sem.at[0])
+    fetch = pltpu.make_async_copy(meta_ref, num_ref, sem)
     fetch.start()
-    for move in moves:
-        move.start()
     for box in range(3 * top_count):
         box_ref[box] = -1
+    lift_groups((far_ref,), dense_ref, last_ref, rows)
     fetch.wait()
-    sids = [num_ref[5, s] for s in range(group)]
-    raise_group(far_ref, sids, idx_ref, val_ref, shift_ref, top_ref, 2 * group, rows)
     boxes = [
         num_ref[2 * (s // group), s % group] + bases[s // group] * top_count for s in range(leaves)
     ]
@@ -261,8 +219,20 @@
         return carry
 
     lax.fori_loop(0, group, listing, 0)
-    for move in moves:
-        move.wait()
+
+    def shifted(b, carry):
+        start = pl.multiple_of(b * block, block)
+        for s in range(leaves):
+            ref, line = (lifted_ref, s * 16) if s < 2 * group else (last_ref, (s - 2 * group) * 16)
+            real = ref[line : line + 8, pl.ds(start, block)]
+            imag = ref[line + 8 : line + 16, pl.ds(start, block)]
+            sid = 2 * num_ref[2 * (s // group) + 1, s % group]
+            shift_real, shift_imag = shift_ref[sid, b], shift_ref[sid + 1, b]
+            top_ref[s, 0, b] = real * shift_real - imag * shift_imag
+            top_ref[s, 1, b] = real * shift_imag + imag * shift_real
+        return carry
+
+    lax.fori_loop(0, local_blocks, shifted, 0)
 
     def merge(s, carry):
         rep = rep_ref[s]
@@ -438,25 +408,22 @@
     beyond = lax.ppermute(here, ("box", "samp"), swap)
     shift_rows = shift_table.astype(F32).reshape(-1, local_blocks, block)
     trans_rows = trans_table.astype(F32).reshape(-1, local_blocks, block)
-    up_shape = pltpu.VMEM((group, 2, local_blocks, 8, block), F32)
-    work = 2 * group * 16 * 2 * block * local_blocks * block
-    values, dense, wide_shift, wide_trans, here_up = pl.pallas_call(
-        functools.partial(tables_kernel, rows=rows),
+    work = 2 * leaves * 16 * in_blocks * block * local_blocks * block
+    dense, wide_shift, wide_trans = pl.pallas_call(
+        tables_kernel,
         out_shape=[
-            pltpu.VMEM(interp_val.shape, BF16),
             pltpu.VMEM((local_blocks * block, in_blocks * block), BF16),
             pltpu.VMEM((shift_rows.shape[0], local_blocks, 8, block), F32),
             pltpu.VMEM((trans_rows.shape[0], local_blocks, 8, block), F32),
-            up_shape,
         ],
-        in_specs=[SMEM, SMEM, VMEM, HBM, VMEM, VMEM],
-        out_specs=[VMEM] * 5,
-        scratch_shapes=[pltpu.SemaphoreType.DMA],
+        in_specs=[SMEM, HBM, VMEM, VMEM],
+        out_specs=[VMEM] * 3,
+        scratch_shapes=[pltpu.VMEM(interp_val.shape, BF16), pltpu.SemaphoreType.DMA],
         compiler_params=params(),
         cost_estimate=pl.CostEstimate(flops=work, bytes_accessed=1 << 24, transcendentals=0),
         name="tables",
-    )(interp_idx, leaf_shift, here, *pinned(interp_val), shift_rows, trans_rows)
-    beyond, values = lax.optimization_barrier((beyond, values))
+    )(interp_idx, *pinned(interp_val), shift_rows, trans_rows)
+    beyond, dense = lax.optimization_barrier((beyond, dense))
     if n_samp == 2:
         first = beyond
         second = lax.ppermute(beyond, "samp", [(0, 1), (1, 0)])
@@ -464,24 +431,24 @@
         ends = lax.all_gather(beyond, "samp", axis=0)
         first, second = ends[0], ends[n_samp - 1]
     numbers = [pltpu.VMEM((8, block), jnp.int32), pltpu.SMEM((8, block), jnp.int32)]
-    first_up = pl.pallas_call(
-        functools.partial(raise_kernel, rows=rows),
-        out_shape=up_shape,
-        in_specs=[SMEM] + [VMEM] * 3,
+    lifted = pl.pallas_call(
+        functools.partial(lift_kernel, rows=rows),
+        out_shape=pltpu.VMEM((2 * group * 16, local_blocks * block), F32),
+        in_specs=[VMEM] * 3,
         out_specs=VMEM,
-        scratch_shapes=numbers + [pltpu.SemaphoreType.DMA],
         compiler_params=params(),
         cost_estimate=pl.CostEstimate(flops=work, bytes_accessed=1 << 23, transcendentals=0),
-        name="raise",
-    )(interp_idx, first, values, wide_shift)
+        name="lift",
+    )(here, first, dense)
 
     fars = pl.pallas_call(
         functools.partial(field_kernel, n_samp=n_samp, leaf_count=leaf_count, tile=tile),
         out_shape=[jax.ShapeDtypeStruct((in_blocks, rows, block), BF16)] * n_samp,
-        in_specs=[SMEM] * 5 + [VMEM] * 9,
+        in_specs=[SMEM] * 4 + [VMEM] * 7,
         out_specs=[VMEM] * n_samp,
         scratch_shapes=[
             pltpu.VMEM((leaves, 2, local_blocks, 8, block), F32),
+            pltpu.VMEM((group * 16, local_blocks * block), F32),
             pltpu.VMEM((group, 2, local_blocks, 8, block), F32),
             pltpu.VMEM((group * 16, local_blocks * block), BF16),
             pltpu.VMEM((group * 16, in_blocks * block), F32),
@@ -491,12 +458,11 @@
             pltpu.SMEM((group,), jnp.int32),
             pltpu.SMEM((group, entries), jnp.int32),
             pltpu.SMEM((group, entries), jnp.int32),
-            pltpu.SemaphoreType.DMA((3,)),
+            pltpu.SemaphoreType.DMA,
         ],
         compiler_params=params(),
         name="field",
     )(
-        interp_idx,
         leaf_parent,
         leaf_shift,
         top_src,
@@ -504,9 +470,7 @@
         here,
         first,
         second,
-        first_up,
-        here_up,
-        values,
+        lifted,
         dense,
         wide_shift,
         wide_trans,

time: 32.6 us -> 29 us (0.89)
  the two profiles are of different devices: /device:TPU:15 before, /device:TPU:11 now
where the time goes in v1:
time: 29 us; the launch traced here: 28.9 us
  Pallas kernels  21.1 us (73%)
  starting transfers between devices  3.92 us (14%)
  blocking collectives  2.24 us (8%)
  waiting for transfers between devices  0.91 us (3%)
  local copies, waits for them, and re-layouts  0.56 us (2%)
    pallas_call x1, Pallas kernels, per_device(): pl.pallas_call(functools.partial(field_kernel, n_samp=n_samp, leaf_count=...  10.5 us
    pallas_call x1, Pallas kernels, per_device(): pl.pallas_call(tables_kernel, out_shape=[pltpu.VMEM((local_blocks * block...  4.26 us
    ppermute x1, starting transfers between devices, per_device(): beyond = lax.ppermute(here, ('box', 'samp'), swap)  3.35 us
    all_gather x1, blocking collectives, per_device(): here = lax.all_gather(message, 'samp', axis=0)  2.24 us
    pallas_call x1, Pallas kernels, per_device(): pl.pallas_call(functools.partial(radiate_kernel, top_count=top_count), ou...  2.2 us
    pallas_call x1, Pallas kernels, per_device(): pl.pallas_call(functools.partial(near_kernel, rows=rows, n_samp=n_samp),...  1.79 us
    pallas_call x1, Pallas kernels, per_device(): pl.pallas_call(functools.partial(lift_kernel, rows=rows), out_shape=pltpu...  1.29 us
    pallas_call x1, Pallas kernels, per_device(): pl.pallas_call(receive_kernel, out_shape=jax.ShapeDtypeStruct((leaf_count...  1 us
  transfers between devices with their start and end apart: 3, of which 2 were waited for; matrix products, arithmetic and copies ran while one was open for 2% of the time, Pallas kernels for 25%

profile of v1, /device:TPU:11, one launch (start us, length us, event | category | flops | bytes accessed | tf_op | source)
XLA Modules:
  0.0 28.9 jit_solution(18424166088561798734)
XLA Ops:
  0.0 0.0 copy-start.7
  0.0 0.0 copy-start.8
  0.0 0.0 copy-start.9
  0.0 2.2 %radiate.1 = bf16[4,80,128]{2,1,0:T(8,128)(2,1)S(1)} custom-call(s32[8]{0:T(128)} %parent_ref.1, s32[8]{0:T(128)} %sid_ref.1, bf16[4,8,128]{2,1,0:T(8,128)(2,1)} %cur_hbm.1, bf16[4,2,2,512,128]{4,3,2,1,0:T(8,128)(2,1)} %rad_ref.1), custom_call_target="tpu_custom_call" | custom-call | tf_op jit(solution)/shard_map/radiate/pallas_call | solution.py:386
  2.2 2.2 %all-gather = bf16[8,80,128]{2,1,0:T(8,128)(2,1)S(1)} all-gather(bf16[4,80,128]{2,1,0:T(8,128)(2,1)S(1)} %radiate.1), channel_id=2, replica_groups=mesh['box'=16,'samp'=2] {'samp'}, dimensions={0}, use_global_device_ids=true | all-gather | bytes 245760 | tf_op jit(solution)/shard_map/all_gather | solution.py:402
  4.5 3.3 %collective-permute-start = (bf16[2,4,80,128]{3,2,1,0:T(8,128)(2,1)S(1)}, bf16[2,4,80,128]{3,2,1,0:T(8,128)(2,1)S(1)}, u32[]{:S(2)}, u32[]{:S(2)}) collective-permute-start(bf16[2,4,80,128]{3,2,1,0:T(8,128)(2,1)S(1)} %bitcast.1), channel_id=1, source_target_pairs={{1,2},{2,1},{3,4},{4,3},{5,6},{6,5},{7,8},{8,7},{9,10},{10,9},{11,... | collective-permute-start | bytes 491528 | tf_op jit(solution)/shard_map/ppermute | solution.py:408
  7.8 0.0 copy-done.7
  7.8 0.3 %reshape.17.trans_ref = f32[64,32,128]{2,1,0:T(8,128)S(1)} reshape(bf16[32,2,4096]{2,1,0:T(2,128)(2,1)S(1)} %copy-done.7) | data formatting | bytes 1572864 | tf_op jit(solution)/shard_map/reshape | solution.py:410
  8.2 0.0 copy-done.8
  8.2 0.1 reshape.15.shift_ref
  8.3 0.0 copy-done.9
  8.3 0.1 copy.14.idx_ref
  8.4 4.3 %tables.1 = (bf16[4096,512]{1,0:T(8,128)(2,1)S(1)}, f32[16,32,8,128]{3,2,1,0:T(8,128)S(1)}, f32[64,32,8,128]{3,2,1,0:T(8,128)S(1)}) custom-call(s32[32,2]{1,0:T(8,128)S(1)} %copy.14.idx_ref, bf16[32,2,128,128]{3,2,1,0:T(8,128)(2,1)} %val_hbm.1, f32[16,32,128]{2,1,0:T(8,128)S(1)} %reshape.15.shift_ref, f32[64,32,128]{2,1,0:T(8,128)S(1)} %reshape.17.trans_ref), custom_call_target="tpu_custom_call" | custom-call | flops 1610612736 | bytes 16777216 | tf_op jit(solution)/shard_map/tables/pallas_call | solution.py:412
  12.7 0.8 %collective-permute-done.first_ref.near_ref = bf16[2,4,80,128]{3,2,1,0:T(8,128)(2,1)S(1)} collective-permute-done((bf16[2,4,80,128]{3,2,1,0:T(8,128)(2,1)S(1)}, bf16[2,4,80,128]{3,2,1,0:T(8,128)(2,1)S(1)}, u32[]{:S(2)}, u32[]{:S(2)}) %collective-permute-start) | collective-permute-done | bytes 163872 | tf_op jit(solution)/shard_map/ppermute | solution.py:408
  13.5 0.1 collective-permute-start.1
  13.6 1.3 %lift.1.lifted_ref = f32[256,4096]{1,0:T(8,128)S(1)} custom-call(bf16[2,4,80,128]{3,2,1,0:T(8,128)(2,1)S(1)} %bitcast.2, bf16[2,4,80,128]{3,2,1,0:T(8,128)(2,1)S(1)} %collective-permute-done.first_ref.near_ref, bf16[4096,512]{1,0:T(8,128)(2,1)S(1)} %get-tuple-element.14.dense_ref), custom_call_target="tpu_custom_call" | custom-call | flops 1610612736 | bytes 8388608 | tf_op jit(solution)/shard_map/lift/pallas_call | solution.py:434
  14.9 0.1 collective-permute-done.1.second_ref.far_ref
  14.9 0.0 copy-done.2
  14.9 0.0 copy-done.3
  14.9 0.0 copy-done.5
  15.0 0.0 copy-done.6
  15.0 0.0 copy-start.1
  15.0 0.0 copy-start.4
  15.0 10.5 %field.1 = (bf16[4,64,128]{2,1,0:T(8,128)(2,1)S(1)}, bf16[4,64,128]{2,1,0:T(8,128)(2,1)S(1)}) custom-call(s32[8]{0:T(128)S(1)} %copy-done.5, s32[8]{0:T(128)S(1)} %copy-done.6, s32[16,16]{1,0:T(8,128)S(1)} %copy-done.2, s32[16,16]{1,0:T(8,128)S(1)} %copy-done.3, bf16[2,4,80,128]{3,2,1,0:T(8,128)(2,1)S(1)} %bitcast.3, ...), custom_call_target="tpu_custom_call" | custom-call | tf_op jit(solution)/shard_map/field/pallas_call | solution.py:444
  25.5 0.0 copy-start
  25.6 0.5 %collective-permute-start.2 = (bf16[4,64,128]{2,1,0:T(8,128)(2,1)S(1)}, bf16[4,64,128]{2,1,0:T(8,128)(2,1)S(1)}, u32[]{:S(2)}, u32[]{:S(2)}) collective-permute-start(bf16[4,64,128]{2,1,0:T(8,128)(2,1)S(1)} %get-tuple-element.18), channel_id=1, source_target_pairs={{0,1},{1,0},{2,3},{3,2},{4,5},{5,4},{6,7},{7,6},{8,9},{9,8},{10,11... | collective-permute-start | bytes 196616 | tf_op jit(solution)/shard_map/ppermute | solution.py:479
  26.1 0.0 copy-done.1
  26.1 0.0 copy-done.4
  26.1 1.8 %near.1.near_ref = f32[4,8,128]{2,1,0:T(8,128)S(1)} custom-call(s32[4,8]{1,0:T(4,128)S(1)} %copy-done.4, bf16[2,4,80,128]{3,2,1,0:T(8,128)(2,1)S(1)} %bitcast.4, bf16[2,4,80,128]{3,2,1,0:T(8,128)(2,1)S(1)} %collective-permute-done.first_ref.near_ref, bf16[2,4,80,128]{3,2,1,0:T(8,128)(2,1)S(1)} %collective-permute-done.1.second_ref.far_ref, ...), custom_call_target="tpu_custom_call" | custom-call | tf_op jit(solution)/shard_map/near/pallas_call | solution.py:482
  27.9 0.0 collective-permute-done.2.rest_1_
  27.9 0.0 copy-done
  27.9 1.0 %receive.1 = f32[4,8,128]{2,1,0:T(8,128)} custom-call(f32[4,8,128]{2,1,0:T(8,128)S(1)} %near.1.near_ref, bf16[4,2,2,512,128]{4,3,2,1,0:T(8,128)(2,1)S(1)} %copy-done, bf16[4,64,128]{2,1,0:T(8,128)(2,1)S(1)} %get-tuple-element.17.rest_0_, bf16[4,64,128]{2,1,0:T(8,128)(2,1)S(1)} %collective-permute-done.2.rest_1_), custom_call_target="tpu_custom_call" | custom-call | tf_op jit(solution)/shard_map/receive/pallas_call | solution.py:495
  (4 shorter events, 0.0 us)
Async XLA Ops:
  0.0 7.8 %copy-start.7 = (bf16[32,2,4096]{2,1,0:T(2,128)(2,1)S(1)}, bf16[32,2,4096]{2,1,0:T(2,128)(2,1)}, u32[]{:S(2)}) copy-start(bf16[32,2,4096]{2,1,0:T(2,128)(2,1)} %param.23) | copy-start | bytes 1572868
  0.0 8.2 %copy-start.8 = (bf16[8,2,4096]{2,1,0:T(2,128)(2,1)S(1)}, bf16[8,2,4096]{2,1,0:T(2,128)(2,1)}, u32[]{:S(2)}) copy-start(bf16[8,2,4096]{2,1,0:T(2,128)(2,1)} %param.18) | copy-start | bytes 393220
  0.0 8.3 %copy-start.9 = (s32[32,2]{0,1:T(2,128)S(1)}, s32[32,2]{0,1:T(2,128)}, u32[]{:S(2)}) copy-start(s32[32,2]{0,1:T(2,128)} %param.19) | copy-start | bytes 772
  4.5 9.0 %collective-permute-start = (bf16[2,4,80,128]{3,2,1,0:T(8,128)(2,1)S(1)}, bf16[2,4,80,128]{3,2,1,0:T(8,128)(2,1)S(1)}, u32[]{:S(2)}, u32[]{:S(2)}) collective-permute-start(bf16[2,4,80,128]{3,2,1,0:T(8,128)(2,1)S(1)} %bitcast.1), channel_id=1, source_target_pairs={{1,2},{2,1},{3,4},{4,3},{5,6},{6,5},{7,8},{8,7},{9,10},{10,9},{11,... | collective-permute-start | bytes 491528 | tf_op jit(solution)/shard_map/ppermute | solution.py:408
  13.5 1.5 %copy-start.2 = (s32[16,16]{1,0:T(8,128)S(1)}, s32[16,16]{1,0:T(8,128)}, u32[]{:S(2)}) copy-start(s32[16,16]{1,0:T(8,128)} %src_ref.3) | copy-start | bytes 3076
  13.5 1.5 %copy-start.3 = (s32[16,16]{1,0:T(8,128)S(1)}, s32[16,16]{1,0:T(8,128)}, u32[]{:S(2)}) copy-start(s32[16,16]{1,0:T(8,128)} %disp_ref.1) | copy-start | bytes 3076
  13.5 1.5 %copy-start.5 = (s32[8]{0:T(128)S(1)}, s32[8]{0:T(128)}, u32[]{:S(2)}) copy-start(s32[8]{0:T(128)} %parent_ref.1) | copy-start | bytes 100
  13.5 1.5 %copy-start.6 = (s32[8]{0:T(128)S(1)}, s32[8]{0:T(128)}, u32[]{:S(2)}) copy-start(s32[8]{0:T(128)} %sid_ref.1) | copy-start | bytes 100
  13.5 1.5 %collective-permute-start.1 = (bf16[2,4,80,128]{3,2,1,0:T(8,128)(2,1)S(1)}, bf16[2,4,80,128]{3,2,1,0:T(8,128)(2,1)S(1)}, u32[]{:S(2)}, u32[]{:S(2)}) collective-permute-start(bf16[2,4,80,128]{3,2,1,0:T(8,128)(2,1)S(1)} %collective-permute-done.first_ref.near_ref), channel_id=1, source_target_pairs={{0,1},{1,0},{2,3},{3,2},{4,5},{5,4},{6,7},{7,6},{8,9},{9,8},{10,11... | collective-permute-start | bytes 491528 | tf_op jit(solution)/shard_map/ppermute | solution.py:429
  15.0 11.1 %copy-start.1 = (bf16[4,8,2,128,128]{4,3,2,1,0:T(8,128)(2,1)S(1)}, bf16[4,8,2,128,128]{4,3,2,1,0:T(8,128)(2,1)}, u32[]{:S(2)}) copy-start(bf16[4,8,2,128,128]{4,3,2,1,0:T(8,128)(2,1)} %near_hbm.1) | copy-start | bytes 6291460
  15.0 11.1 %copy-start.4 = (s32[4,8]{1,0:T(4,128)S(1)}, s32[4,8]{1,0:T(4,128)}, u32[]{:S(2)}) copy-start(s32[4,8]{1,0:T(4,128)} %src_ref.2) | copy-start | bytes 388
  25.5 2.3 %copy-start = (bf16[4,2,2,512,128]{4,3,2,1,0:T(8,128)(2,1)S(1)}, bf16[4,2,2,512,128]{4,3,2,1,0:T(8,128)(2,1)}, u32[]{:S(2)}) copy-start(bf16[4,2,2,512,128]{4,3,2,1,0:T(8,128)(2,1)} %rad_ref.1) | copy-start | bytes 6291460
  25.6 2.3 %collective-permute-start.2 = (bf16[4,64,128]{2,1,0:T(8,128)(2,1)S(1)}, bf16[4,64,128]{2,1,0:T(8,128)(2,1)S(1)}, u32[]{:S(2)}, u32[]{:S(2)}) collective-permute-start(bf16[4,64,128]{2,1,0:T(8,128)(2,1)S(1)} %get-tuple-element.18), channel_id=1, source_target_pairs={{0,1},{1,0},{2,3},{3,2},{4,5},{5,4},{6,7},{7,6},{8,9},{9,8},{10,11... | collective-permute-start | bytes 196616 | tf_op jit(solution)/shard_map/ppermute | solution.py:479
